TPU v7x, 32 devices: a whole 2x2x4 slice. The times are simulated.
32 devices in a mesh: dp: 4 (over z), sp: 8 (over y, x, core).
Axes of the slice: x: 2, y: 2, z: 4, core: 2. Of those that a mesh axis runs over, the one named last changes fastest.
Arguments:
- projected: bfloat16 [4096, 10240], P(('dp', 'sp')), may hold values from -4 to 4
- bias: float32 [10240], replicated, may hold values from -3 to 3
- cotangent: bfloat16 [4096, 8192], P(('dp', 'sp')), may hold values from -4 to 4
- lengths: int32 [4, 4], P('dp'), may hold values from 1 to 512, 1024 in all within a row
- page_source: int32 [4, 64], P('dp'), may hold values from 0 to 63, as said below
Outputs:
- attended: bfloat16 [4096, 8192], P(('dp', 'sp'))
- grad_query: bfloat16 [4096, 8192], P(('dp', 'sp'))
- key_value_gradient: bfloat16 [4096, 2048], P(('dp', 'sp'))
- grad_bias: float32 [10240], replicated
Inputs may be any that keep to these rules, and one draw needn't show every extreme that they name: Each row holds the lengths of the 4 sequences of one group in packed order and sums to 1024; the longest is exactly 512. `page_source`: rollout page r of a group lies on the group's device r // 8 at slot r % 8. Each row is a permutation of the group's pages, and no device sends two pages to the same device of its group.
All inputs are finite; a program needn't handle non-finite values.
Results may differ from a plain program's by a relative error of at most 0.012.
Values may be sent and summed in bfloat16 or wider, within the bound.
A program may use at most 192 MiB of HBM per device.

v0:
```python
import functools

import jax
import jax.numpy as jnp
from jax import lax
from jax.experimental import pallas as pl
from jax.experimental.pallas import tpu as pltpu
from jax.sharding import PartitionSpec as P

QUERY_HEADS = 64
KEY_VALUE_HEADS = 8
HEAD_DIMENSION = 128
PAGE = 16
QBLK = 512


rope_base = 1000000.0


def rope_tables(positions, head_size):
    half_size = head_size // 2
    exponent = jnp.arange(half_size, dtype=jnp.float32) * 2.0 / head_size
    frequency = jnp.power(jnp.float32(rope_base), -exponent)
    angles = positions.astype(jnp.float32)[:, None] * frequency[None, :]
    cosine_table = jnp.cos(angles)
    sine_table = jnp.sin(angles)
    return (
        jnp.concatenate([cosine_table, cosine_table], 1),
        jnp.concatenate([sine_table, sine_table], 1),
    )


def turn_half(tensor_in):
    half_size = tensor_in.shape[-1] // 2
    return jnp.concatenate([-tensor_in[..., half_size:], tensor_in[..., :half_size]], -1)


def apply_rotary(tensor_in, cosine_table, sine_table):
    return tensor_in * cosine_table[:, None, :] + turn_half(tensor_in) * sine_table[:, None, :]


def unrotate(tensor_in, cosine_table, sine_table):
    return tensor_in * cosine_table[:, None, :] - turn_half(tensor_in) * sine_table[:, None, :]


def segments_of(seq_lengths, token_total_count):
    seq_ends = jnp.cumsum(seq_lengths)
    seq_starts = seq_ends - seq_lengths
    tokens_at = jnp.arange(token_total_count, dtype=jnp.int32)
    segment = jnp.sum((tokens_at[:, None] >= seq_ends[None, :]).astype(jnp.int32), 1)
    labels = jnp.arange(seq_lengths.shape[0], dtype=jnp.int32)
    first_token = jnp.sum(jnp.where(segment[:, None] == labels[None, :], seq_starts[None, :], 0), 1)
    return (segment, tokens_at - first_token, first_token)


def shards(projected, bias, cotangent, lengths, page_source):
    shard_rows, row_width = projected.shape
    partition_count = lax.axis_size("sp")
    my_index = lax.axis_index("sp")
    group_rows = shard_rows * partition_count
    pages_dev = shard_rows // PAGE
    query_span_width = QUERY_HEADS * HEAD_DIMENSION
    key_value_width = KEY_VALUE_HEADS * HEAD_DIMENSION
    heads_dev = QUERY_HEADS // partition_count
    head_copies = partition_count // KEY_VALUE_HEADS
    page_table = page_source[0]
    page_grid = page_table.reshape(partition_count, pages_dev)
    source_dev = page_grid // pages_dev
    source_slot = page_grid % pages_dev
    from_here = source_dev == my_index
    pick_slot = jnp.sum(jnp.where(from_here, source_slot, 0), 1)
    present = jnp.any(from_here, 1)
    local_pages = projected.reshape(pages_dev, PAGE, row_width)
    outgoing = jnp.where(
        present[:, None, None], local_pages[pick_slot], jnp.zeros((), projected.dtype)
    )
    incoming = lax.all_to_all(outgoing, "sp", split_axis=0, concat_axis=0, tiled=True)
    own_sources = lax.dynamic_slice_in_dim(source_dev, my_index, 1, 0)[0]
    trainer_rows = incoming[own_sources].reshape(shard_rows, row_width)
    query_part = trainer_rows[:, :query_span_width]
    key_part = trainer_rows[:, query_span_width : query_span_width + key_value_width].reshape(
        shard_rows, KEY_VALUE_HEADS, 1, HEAD_DIMENSION
    )
    value_portion = trainer_rows[:, query_span_width + key_value_width :].reshape(
        shard_rows, KEY_VALUE_HEADS, 1, HEAD_DIMENSION
    )
    joined_rows = jnp.concatenate([key_part, value_portion], 3)
    repeated_heads = jnp.broadcast_to(
        joined_rows, (shard_rows, KEY_VALUE_HEADS, head_copies, 2 * HEAD_DIMENSION)
    ).reshape(shard_rows, partition_count * 2 * HEAD_DIMENSION)
    head_query, head_pair, head_upstream = (
        lax.all_to_all(query_part, "sp", split_axis=1, concat_axis=0, tiled=True),
        lax.all_to_all(repeated_heads, "sp", split_axis=1, concat_axis=0, tiled=True),
        lax.all_to_all(cotangent, "sp", split_axis=1, concat_axis=0, tiled=True),
    )
    kv_head = my_index // head_copies
    query_bias = lax.dynamic_slice_in_dim(
        bias, my_index * heads_dev * HEAD_DIMENSION, heads_dev * HEAD_DIMENSION
    )
    key_bias = lax.dynamic_slice_in_dim(
        bias, query_span_width + kv_head * HEAD_DIMENSION, HEAD_DIMENSION
    )
    value_bias = lax.dynamic_slice_in_dim(
        bias, query_span_width + key_value_width + kv_head * HEAD_DIMENSION, HEAD_DIMENSION
    )
    segment, position, first_token = segments_of(lengths[0], group_rows)
    cosine_table, sine_table = rope_tables(position, HEAD_DIMENSION)
    query_matrix = head_query.astype(jnp.float32).reshape(
        group_rows, heads_dev, HEAD_DIMENSION
    ) + query_bias.reshape(heads_dev, HEAD_DIMENSION)
    query_matrix = apply_rotary(query_matrix, cosine_table, sine_table).astype(jnp.bfloat16)
    key_rows = head_pair[:, :HEAD_DIMENSION].astype(jnp.float32) + key_bias
    key_rows = apply_rotary(key_rows[:, None, :], cosine_table, sine_table)[:, 0].astype(
        jnp.bfloat16
    )
    value_rows = (head_pair[:, HEAD_DIMENSION:].astype(jnp.float32) + value_bias).astype(
        jnp.bfloat16
    )
    block_count = group_rows // QBLK
    score_scale = HEAD_DIMENSION ** (-0.5)
    query_blocks = query_matrix.reshape(block_count, QBLK, heads_dev, HEAD_DIMENSION)
    key_blocks = key_rows.reshape(block_count, QBLK, HEAD_DIMENSION)
    value_blocks = value_rows.reshape(block_count, QBLK, HEAD_DIMENSION)
    segment_blocks = segment.reshape(block_count, QBLK)
    token_blocks = jnp.arange(group_rows, dtype=jnp.int32).reshape(block_count, QBLK)
    upstream_gradient = head_upstream.reshape(block_count, QBLK, heads_dev, HEAD_DIMENSION)

    def weights(row_block, col_block):
        scores = (
            jnp.einsum(
                "qhd,kd->hqk",
                query_blocks[row_block],
                key_blocks[col_block],
                preferred_element_type=jnp.float32,
            )
            * score_scale
        )
        keep = (segment_blocks[row_block][:, None] == segment_blocks[col_block][None, :]) & (
            token_blocks[row_block][:, None] >= token_blocks[col_block][None, :]
        )
        return jnp.where(keep[None], jnp.exp(scores), 0.0)

    zero_rows = jnp.zeros((heads_dev, QBLK), jnp.float32)
    totals = []
    for row_block in range(block_count):
        running = zero_rows
        for col_block in range(row_block + 1):
            running = running + jnp.sum(weights(row_block, col_block), 2)
        totals.append(running)
    zero_out = jnp.zeros((QBLK, heads_dev, HEAD_DIMENSION), jnp.float32)
    attended_blocks = []
    for row_block in range(block_count):
        running = zero_out
        for col_block in range(row_block + 1):
            attend_probs = (weights(row_block, col_block) / totals[row_block][:, :, None]).astype(
                jnp.bfloat16
            )
            running = running + jnp.einsum(
                "hqk,kd->qhd",
                attend_probs,
                value_blocks[col_block],
                preferred_element_type=jnp.float32,
            )
        attended_blocks.append(running.astype(jnp.bfloat16))
    attended = jnp.stack(attended_blocks)
    attended_out = lax.all_to_all(
        attended.reshape(group_rows, heads_dev * HEAD_DIMENSION),
        "sp",
        split_axis=0,
        concat_axis=1,
        tiled=True,
    )
    zero_key = jnp.zeros((QBLK, HEAD_DIMENSION), jnp.float32)
    key_grads = [zero_key for col_block in range(block_count)]
    value_grads = [zero_key for col_block in range(block_count)]
    query_grads = []
    for row_block in range(block_count):
        delta = jnp.transpose(
            jnp.sum(
                upstream_gradient[row_block].astype(jnp.float32)
                * attended[row_block].astype(jnp.float32),
                2,
            )
        )
        running = zero_out
        for col_block in range(row_block + 1):
            probs = weights(row_block, col_block) / totals[row_block][:, :, None]
            rounded = probs.astype(jnp.bfloat16)
            dprobs = jnp.einsum(
                "qhd,kd->hqk",
                upstream_gradient[row_block],
                value_blocks[col_block],
                preferred_element_type=jnp.float32,
            )
            dscores = (probs * (dprobs - delta[:, :, None])).astype(jnp.bfloat16)
            part_query = (
                jnp.einsum(
                    "hqk,kd->qhd",
                    dscores,
                    key_blocks[col_block],
                    preferred_element_type=jnp.float32,
                )
                * score_scale
            )
            part_key = (
                jnp.einsum(
                    "hqk,qhd->kd",
                    dscores,
                    query_blocks[row_block],
                    preferred_element_type=jnp.float32,
                )
                * score_scale
            )
            part_value = jnp.einsum(
                "hqk,qhd->kd",
                rounded,
                upstream_gradient[row_block],
                preferred_element_type=jnp.float32,
            )
            part_query, part_key, part_value = (part_query, part_key, part_value)
            running = running + part_query
            key_grads[col_block] = key_grads[col_block] + part_key
            value_grads[col_block] = value_grads[col_block] + part_value
        query_grads.append(running)
    rot_query = jnp.stack(query_grads).reshape(group_rows, heads_dev, HEAD_DIMENSION)
    grad_query = (
        unrotate(rot_query, cosine_table, sine_table)
        .astype(jnp.bfloat16)
        .reshape(group_rows, heads_dev * HEAD_DIMENSION)
    )
    query_out = lax.all_to_all(grad_query, "sp", split_axis=0, concat_axis=1, tiled=True)
    grad_key = unrotate(
        jnp.stack(key_grads).reshape(group_rows, 1, HEAD_DIMENSION), cosine_table, sine_table
    ).reshape(group_rows, HEAD_DIMENSION)
    grad_value = jnp.stack(value_grads).reshape(group_rows, HEAD_DIMENSION)
    pair_grads = jnp.concatenate([grad_key, grad_value], 1)
    pair_gradient_back = lax.all_to_all(pair_grads, "sp", split_axis=0, concat_axis=1, tiled=True)
    pair_gradient_sum = jnp.sum(
        pair_gradient_back.reshape(shard_rows, KEY_VALUE_HEADS, head_copies, 2, HEAD_DIMENSION), 2
    )
    key_value_gradient = (
        jnp.transpose(pair_gradient_sum, (0, 2, 1, 3))
        .reshape(shard_rows, 2 * key_value_width)
        .astype(jnp.bfloat16)
    )
    local_sums = jnp.concatenate(
        [
            jnp.sum(query_out.astype(jnp.float32), 0),
            jnp.sum(key_value_gradient.astype(jnp.float32), 0),
        ]
    )
    grad_bias = lax.psum(local_sums, ("dp", "sp"))
    return (attended_out, query_out, key_value_gradient, grad_bias)


MESH = pl.DeviceIdType.MESH
D = HEAD_DIMENSION
NT = (((1,), (1,)), ((), ()))
NN = (((1,), (0,)), ((), ()))


def dot(left, right, dims=NN):
    return lax.dot_general(left, right, dims, preferred_element_type=jnp.float32)


def fused_kernel(
    n, ndp, rows,
    len_ref, page_ref, proj_ref, cot_ref, bias_ref, freq_ref,
    att_out, gq_out, kvg_out, gb_out,
    out_q, out_kv, recv_q, recv_kv, recv_c, perm_out, perm_q, perm_kv,
    key_rows, value_rows, key_t, value_t, cos_t, sin_t, mask_t, att_buf, gq_buf,
    dk, dv, own_kv, part_kv, got_kv, fin_kv, sums, dp_buf, total, gb_all,
    kv_send, kv_recv, q_send, q_recv, c_send, c_recv, c_here,
    o_send, o_recv, o_here, p_send, p_recv, f_send, f_recv, f_here,
    dp_send, dp_recv, gb_send, gb_recv,
):
    me = lax.axis_index("sp")
    mine = lax.axis_index("dp")
    chip, core = me // 2, lax.rem(me, 2)
    chips = n // 2
    tokens = 2 * rows
    group = n * rows
    share = 2 * PAGE
    pages_dev = rows // PAGE
    back = (group // 2 - 1 + tokens - 1) // tokens
    span = (back + 1) * tokens
    home = back * tokens
    half = QUERY_HEADS // 2
    pairs = KEY_VALUE_HEADS // 2
    copies = half // pairs
    wide = copies * D
    scale = D ** (-0.5)
    key_base = QUERY_HEADS * D
    value_base = key_base + KEY_VALUE_HEADS * D
    query_at = slice(home, span)

    def aligned(start, size):
        return pl.ds(pl.multiple_of(start, size), size)

    def columns(start, size):
        return pl.ds(pl.multiple_of(start, D), size)

    def sp_peer(o):
        return lax.rem(me + o, n)

    def dp_peer(o):
        return lax.rem(mine + o, ndp)

    def move(src, dst, send, recv, target):
        return pltpu.make_async_remote_copy(
            src_ref=src, dst_ref=dst, send_sem=send, recv_sem=recv,
            device_id={"sp": target}, device_id_type=MESH,
        )

    def pair_in(kind, j, o):
        peer = sp_peer(o)
        src = out_kv.at[
            kind * KEY_VALUE_HEADS + lax.rem(peer, 2) * pairs + j,
            pl.ds(pl.multiple_of(peer // 2 * share, share), (back + 1) * share), :,
        ]
        dst = recv_kv.at[kind, j, aligned(me * (back + 1) * share, (back + 1) * share), :]
        if o == 0:
            return pltpu.make_async_copy(src, dst, kv_recv.at[kind, j, 0])
        return move(src, dst, kv_send.at[kind, j, o], kv_recv.at[kind, j, o], peer)

    def query_in(j, o):
        peer = sp_peer(o)
        src = out_q.at[
            pl.ds(lax.rem(peer, 2) * half + j * copies, copies), aligned(peer // 2 * share, share), :
        ]
        dst = recv_q.at[pl.ds(j * copies, copies), aligned(me * share, share), :]
        if o == 0:
            return pltpu.make_async_copy(src, dst, q_recv.at[j, 0])
        return move(src, dst, q_send.at[j, o], q_recv.at[j, o], peer)

    def upstream_in(j, here):
        who = core if here else 1 - core
        src = cot_ref.at[:, columns((who * half + j * copies) * D, wide)]
        dst = recv_c.at[aligned(core * rows, rows), columns(j * wide, wide)]
        if here:
            return pltpu.make_async_copy(src, dst, c_here.at[j])
        return move(src, dst, c_send.at[j], c_recv.at[j], 2 * chip + 1 - core)

    def head_out(kind, j, here):
        buf, land = ((att_buf, att_out), (gq_buf, gq_out))[kind]
        who = core if here else 1 - core
        src = buf.at[aligned(who * rows, rows), columns(j * wide, wide)]
        dst = land.at[:, columns((core * half + j * copies) * D, wide)]
        if here:
            return pltpu.make_async_copy(src, dst, o_here.at[kind, j])
        return move(src, dst, o_send.at[kind, j], o_recv.at[kind, j], 2 * chip + 1 - core)

    def part_out(j, w):
        return move(
            part_kv.at[j, w], got_kv.at[j, w], p_send.at[j, w], p_recv.at[j, w],
            2 * (chip - back + w) + core,
        )

    def pair_out(kind, here):
        who = core if here else 1 - core
        src = fin_kv.at[kind, aligned(who * rows, rows), :]
        dst = kvg_out.at[:, columns((kind * KEY_VALUE_HEADS + core * pairs) * D, pairs * D)]
        if here:
            return pltpu.make_async_copy(src, dst, f_here.at[kind])
        return move(src, dst, f_send.at[kind], f_recv.at[kind], 2 * chip + 1 - core)

    def sums_dp(o):
        return pltpu.make_async_remote_copy(
            src_ref=sums, dst_ref=dp_buf.at[mine],
            send_sem=dp_send.at[o], recv_sem=dp_recv.at[o],
            device_id={"dp": dp_peer(o)}, device_id_type=MESH,
        )

    def sums_sp(o):
        return move(total, gb_all.at[me], gb_send.at[o], gb_recv.at[o], sp_peer(o))

    barrier = pltpu.get_barrier_semaphore()
    for o in range(1, n):
        pl.semaphore_signal(barrier, inc=1, device_id={"sp": sp_peer(o)}, device_id_type=MESH)
    for o in range(1, ndp):
        pl.semaphore_signal(barrier, inc=1, device_id={"dp": dp_peer(o)}, device_id_type=MESH)

    def one_hot(length, source):
        sub = lax.broadcasted_iota(jnp.int32, (PAGE, length), 0)
        lane = lax.broadcasted_iota(jnp.int32, (PAGE, length), 1)
        return jnp.where(lane - sub == source, 1.0, 0.0).astype(jnp.bfloat16)

    for d in range(n):
        slot = jnp.int32(0)
        for i in range(pages_dev):
            page = page_ref[0, d * pages_dev + i]
            slot = slot + jnp.where(
                lax.div(page, pages_dev) == me, lax.rem(page, pages_dev) * PAGE, 0
            )
        perm_out[d * PAGE : (d + 1) * PAGE, :] = one_hot(rows, slot)
    out_kv[:, : back * share, :] = jnp.zeros(
        (2 * KEY_VALUE_HEADS, back * share, D), jnp.bfloat16
    )
    pl.semaphore_wait(barrier, n - 1 + ndp - 1)

    for kind in range(2):
        base = (key_base, value_base)[kind]
        ordered = dot(perm_out[...], proj_ref[:, base : base + KEY_VALUE_HEADS * D])
        for i in range(KEY_VALUE_HEADS):
            out_kv[kind * KEY_VALUE_HEADS + i, back * share :, :] = ordered[
                :, i * D : (i + 1) * D
            ].astype(jnp.bfloat16)

    def send_pair(j, carry):
        for kind in range(2):
            for o in range(n):
                pair_in(kind, j, o).start()
        upstream_in(j, True).start()
        upstream_in(j, False).start()
        for side in range(2):
            first = side * half + j * copies
            ordered = dot(perm_out[...], proj_ref[:, columns(first * D, wide)])
            for i in range(copies):
                out_q[first + i] = ordered[:, i * D : (i + 1) * D].astype(jnp.bfloat16)
        for o in range(n):
            query_in(j, o).start()
        return carry

    lax.fori_loop(0, pairs, send_pair, 0)

    starts = []
    begin = jnp.int32(0)
    for s in range(len_ref.shape[1] - 1):
        begin = begin + len_ref[0, s]
        starts.append(begin)

    def first_of(token):
        first = jnp.zeros_like(token)
        for start in starts:
            first = jnp.where(token >= start, start, first)
        return first

    low = (chip - back) * tokens

    def table_block(i, carry):
        at = aligned(i * 128, 128)
        token = lax.broadcasted_iota(jnp.int32, (128, D), 0) + (i * 128 + low)
        lane = lax.broadcasted_iota(jnp.int32, (128, D), 1)
        angle = (token - first_of(token)).astype(jnp.float32) * freq_ref[...]
        cos_t[at, :] = jnp.cos(angle)
        sine = jnp.sin(angle)
        sin_t[at, :] = jnp.where(lane < D // 2, -sine, sine)
        return carry

    lax.fori_loop(0, span // 128, table_block, 0)

    query_token = lax.broadcasted_iota(jnp.int32, (1, tokens), 1) + chip * tokens
    query_first = first_of(query_token)
    for w in range(back + 1):
        key_token = lax.broadcasted_iota(jnp.int32, (tokens, tokens), 0) + (low + w * tokens)
        keep = (key_token >= query_first) & (key_token <= query_token)
        mask_t[w * tokens : (w + 1) * tokens, :] = jnp.where(keep, 0.0, -jnp.inf)
        for i in range(2 * pages_dev):
            at = jnp.maximum((chip - back + w) * 2 * pages_dev + i, 0)
            source = lax.div(page_ref[0, at], pages_dev)
            inner = i // pages_dev * PAGE
            place = pl.ds(w * tokens + i * PAGE, PAGE)
            perm_kv[place, :] = one_hot(
                n * (back + 1) * share, source * ((back + 1) * share) + w * share + inner
            )
            if w == back:
                perm_q[i * PAGE : (i + 1) * PAGE, :] = one_hot(tokens, source * share + inner)

    def rope(x, at):
        return x * cos_t[at, :] + pltpu.roll(x, D // 2, 1) * sin_t[at, :]

    def unrope(x, at):
        return x * cos_t[at, :] - pltpu.roll(x, D // 2, 1) * sin_t[at, :]

    sums[...] = jnp.zeros_like(sums)

    def one_pair(j, carry):
        for kind in range(2):
            for o in range(n):
                copy = pair_in(kind, j, o)
                copy.wait() if o == 0 else copy.wait_recv()
        key_bias = bias_ref[pl.ds(QUERY_HEADS + core * pairs + j, 1), :]
        value_bias = bias_ref[pl.ds(QUERY_HEADS + KEY_VALUE_HEADS + core * pairs + j, 1), :]
        for w in range(back + 1):
            at = slice(w * tokens, (w + 1) * tokens)
            rotated = rope(dot(perm_kv[at, :], recv_kv[0, j]) + key_bias, at)
            key_rows[at, :] = rotated.astype(jnp.bfloat16)
            key_t[:, at] = rotated.T.astype(jnp.bfloat16)
            shifted = dot(perm_kv[at, :], recv_kv[1, j]) + value_bias
            value_rows[at, :] = shifted.astype(jnp.bfloat16)
            value_t[:, at] = shifted.T.astype(jnp.bfloat16)
        dk[...] = jnp.zeros_like(dk)
        dv[...] = jnp.zeros_like(dv)
        for o in range(n):
            copy = query_in(j, o)
            copy.wait() if o == 0 else copy.wait_recv()
        upstream_in(j, True).wait()
        upstream_in(j, False).wait_recv()

        def two_heads(step, inner):
            for part in range(2):
                h = j * copies + step * 2 + part
                cols = columns(h * D, D)
                query_bias = bias_ref[pl.ds(core * half + h, 1), :]
                query = rope(dot(perm_q[...], recv_q[h]) + query_bias, query_at)
                query = query.astype(jnp.bfloat16)
                upstream = recv_c[:, cols]
                upstream_t = upstream.astype(jnp.float32).T
                scores = dot(key_rows[...], query, NT) * scale
                weights = jnp.exp(scores + mask_t[...])
                totals = jnp.sum(weights, 0, keepdims=True)
                shrink = jnp.where(totals > 1e37, 0.015625, 1.0)
                probs = (weights * shrink) * (1.0 / (totals * shrink))
                rounded = probs.astype(jnp.bfloat16)
                attended_t = dot(value_t[...], rounded)
                att_buf[:, cols] = attended_t.T.astype(jnp.bfloat16)
                kept = attended_t.astype(jnp.bfloat16).astype(jnp.float32)
                delta = jnp.sum(upstream_t * kept, 0, keepdims=True)
                dprobs = dot(value_rows[...], upstream, NT)
                dscores = (probs * (dprobs - delta)).astype(jnp.bfloat16)
                grad_query = unrope(dot(key_t[...], dscores).T * scale, query_at)
                grad_query = grad_query.astype(jnp.bfloat16)
                gq_buf[:, cols] = grad_query
                sums[pl.ds(h, 1), :] = jnp.sum(grad_query.astype(jnp.float32), 0, keepdims=True)
                dk[...] += dot(dscores, query)
                dv[...] += dot(rounded, upstream)
            return inner

        lax.fori_loop(0, copies // 2, two_heads, 0)
        for w in range(back):
            at = slice(w * tokens, (w + 1) * tokens)
            part_kv[j, w, 0] = dk[at, :].astype(jnp.bfloat16)
            part_kv[j, w, 1] = dv[at, :].astype(jnp.bfloat16)

            @pl.when(chip - back + w >= 0)
            def _():
                part_out(j, w).start()

        own_kv[j, 0] = dk[home:, :]
        own_kv[j, 1] = dv[home:, :]
        for kind in range(2):
            head_out(kind, j, True).start()
            head_out(kind, j, False).start()
        return carry

    lax.fori_loop(0, pairs, one_pair, 0)

    for j in range(pairs):
        for w in range(back):

            @pl.when(chip + back - w < chips)
            def _():
                part_out(j, w).wait_recv()
                own_kv[j] = own_kv[j] + got_kv[j, w].astype(jnp.float32)

        grad_key = unrope(own_kv[j, 0] * scale, query_at).astype(jnp.bfloat16)
        grad_value = own_kv[j, 1].astype(jnp.bfloat16)
        fin_kv[0, :, j * D : (j + 1) * D] = grad_key
        fin_kv[1, :, j * D : (j + 1) * D] = grad_value
        sums[half + j : half + j + 1, :] = jnp.sum(grad_key.astype(jnp.float32), 0, keepdims=True)
        sums[half + pairs + j : half + pairs + j + 1, :] = jnp.sum(
            grad_value.astype(jnp.float32), 0, keepdims=True
        )
    for o in range(1, ndp):
        sums_dp(o).start()
    for kind in range(2):
        pair_out(kind, True).start()
        pair_out(kind, False).start()
    dp_buf[mine] = sums[...]
    for o in range(1, ndp):
        sums_dp(o).wait()
    running = dp_buf[0]
    for d in range(1, ndp):
        running = running + dp_buf[d]
    total[...] = running
    for o in range(1, n):
        sums_sp(o).start()
    gb_all[me] = running
    for o in range(1, n):
        sums_sp(o).wait()
    for k in range(2):
        running = gb_all[k]
        for c in range(1, chips):
            running = running + gb_all[2 * c + k]
        gb_out[k * half : (k + 1) * half, :] = running[:half]
        at = QUERY_HEADS + k * pairs
        gb_out[at : at + pairs, :] = running[half : half + pairs]
        at = QUERY_HEADS + KEY_VALUE_HEADS + k * pairs
        gb_out[at : at + pairs, :] = running[half + pairs : half + 2 * pairs]

    for kind in range(2):
        pair_out(kind, True).wait()
        pair_out(kind, False).wait()

    def drain(j, carry):
        for o in range(1, n):
            for kind in range(2):
                pair_in(kind, j, o).wait_send()
            query_in(j, o).wait_send()
        upstream_in(j, False).wait_send()
        for kind in range(2):
            head_out(kind, j, True).wait()
            head_out(kind, j, False).wait()
        for w in range(back):

            @pl.when(chip - back + w >= 0)
            def _():
                part_out(j, w).wait_send()

        return carry

    lax.fori_loop(0, pairs, drain, 0)


def fused_shards(projected, bias, cotangent, lengths, page_source):
    rows, _ = projected.shape
    n = lax.axis_size("sp")
    ndp = lax.axis_size("dp")
    tokens = 2 * rows
    group = n * rows
    back = (group // 2 - 1 + tokens - 1) // tokens
    span = (back + 1) * tokens
    half = QUERY_HEADS // 2
    pairs = KEY_VALUE_HEADS // 2
    share = 2 * PAGE
    exponent = jnp.arange(D // 2, dtype=jnp.float32) * 2.0 / D
    frequency = jnp.power(jnp.float32(rope_base), -exponent)
    frequency = jnp.concatenate([frequency, frequency])[None, :]
    sum_rows = half + 2 * pairs
    f32, bf16 = jnp.float32, jnp.bfloat16
    dma = pltpu.SemaphoreType.DMA
    anywhere = pl.BlockSpec(memory_space=pl.ANY)
    scalars = pl.BlockSpec(memory_space=pltpu.SMEM)
    vector = pl.BlockSpec(memory_space=pltpu.VMEM)
    attended, grad_query, pair_gradient, bias_sums = pl.pallas_call(
        functools.partial(fused_kernel, n, ndp, rows),
        out_shape=(
            jax.ShapeDtypeStruct((rows, QUERY_HEADS * D), bf16),
            jax.ShapeDtypeStruct((rows, QUERY_HEADS * D), bf16),
            jax.ShapeDtypeStruct((rows, 2 * KEY_VALUE_HEADS * D), bf16),
            jax.ShapeDtypeStruct((QUERY_HEADS + 2 * KEY_VALUE_HEADS, D), f32),
        ),
        in_specs=[scalars, scalars, vector, anywhere, vector, vector],
        out_specs=(anywhere, anywhere, anywhere, vector),
        scratch_shapes=[
            pltpu.VMEM((QUERY_HEADS, rows, D), bf16),
            pltpu.VMEM((2 * KEY_VALUE_HEADS, back * share + rows, D), bf16),
            pltpu.VMEM((half, tokens, D), bf16),
            pltpu.VMEM((2, pairs, n * (back + 1) * share, D), bf16),
            pltpu.VMEM((tokens, half * D), bf16),
            pltpu.VMEM((rows, rows), bf16),
            pltpu.VMEM((tokens, tokens), bf16),
            pltpu.VMEM((span, n * (back + 1) * share), bf16),
            pltpu.VMEM((span, D), bf16),
            pltpu.VMEM((span, D), bf16),
            pltpu.VMEM((D, span), bf16),
            pltpu.VMEM((D, span), bf16),
            pltpu.VMEM((span, D), f32),
            pltpu.VMEM((span, D), f32),
            pltpu.VMEM((span, tokens), f32),
            pltpu.VMEM((tokens, half * D), bf16),
            pltpu.VMEM((tokens, half * D), bf16),
            pltpu.VMEM((span, D), f32),
            pltpu.VMEM((span, D), f32),
            pltpu.VMEM((pairs, 2, tokens, D), f32),
            pltpu.VMEM((pairs, back, 2, tokens, D), bf16),
            pltpu.VMEM((pairs, back, 2, tokens, D), bf16),
            pltpu.VMEM((2, tokens, pairs * D), bf16),
            pltpu.VMEM((sum_rows, D), f32),
            pltpu.VMEM((ndp, sum_rows, D), f32),
            pltpu.VMEM((sum_rows, D), f32),
            pltpu.VMEM((n, sum_rows, D), f32),
            dma((2, pairs, n)), dma((2, pairs, n)), dma((pairs, n)), dma((pairs, n)),
            dma((pairs,)), dma((pairs,)), dma((pairs,)),
            dma((2, pairs)), dma((2, pairs)), dma((2, pairs)),
            dma((pairs, back)), dma((pairs, back)),
            dma((2,)), dma((2,)), dma((2,)),
            dma((ndp,)), dma((ndp,)), dma((n,)), dma((n,)),
        ],
        compiler_params=pltpu.CompilerParams(
            collective_id=0, has_side_effects=True, vmem_limit_bytes=56 * 1024 * 1024
        ),
        cost_estimate=pl.CostEstimate(
            flops=14 * half * tokens * span * D,
            bytes_accessed=4 * rows * 36864,
            transcendentals=half * tokens * span,
        ),
    )(lengths, page_source, projected, cotangent, bias.reshape(-1, D), frequency)
    return attended, grad_query, pair_gradient, bias_sums.reshape(-1)


def solution(mesh):
    in_specs = (P(("dp", "sp"), None), P(), P(("dp", "sp"), None), P("dp", None), P("dp", None))
    out_specs = (P(("dp", "sp"), None), P(("dp", "sp"), None), P(("dp", "sp"), None), P())
    body = fused_shards if mesh.shape["sp"] == KEY_VALUE_HEADS else shards
    return jax.shard_map(body, mesh=mesh, in_specs=in_specs, out_specs=out_specs, check_vma=False)
```

profile of v0, /device:TPU:0, one launch (start us, length us, event | category | flops | bytes accessed | tf_op | source)
XLA Modules:
  0.0 91.5 jit_solution(11765631411305950554)
XLA Ops:
  0.6 0.6 maximum_bitcast_fusion.freq_ref
  1.2 84.2 %shard_map.84 = (bf16[128,8192]{1,0:T(8,128)(2,1)}, bf16[128,8192]{1,0:T(8,128)(2,1)}, bf16[128,2048]{1,0:T(8,128)(2,1)}, f32[80,128]{1,0:T(8,128)}) custom-call(s32[1,4]{1,0:T(1,128)} %len_ref.1, s32[1,64]{1,0:T(1,128)} %page_ref.1, bf16[128,10240]{1,0:T(8,128)(2,1)} %proj_ref.1, bf16[128,8192]{1,0:T(8,128)(2,1)} %cot_ref.1, f32[80,128]{1,0:T(8,128)} %bitcast.5, ...), custom_call_target="tpu_custom_call" | custom-call | flops 11274289152 | bytes 18874368 | tf_op jit(solution)/shard_map/pallas_call | solution.py:635
  85.4 0.0 copy-start
  85.4 3.2 %copy.13 = bf16[128,8192]{1,0:T(8,128)(2,1)} copy(bf16[128,8192]{1,0:T(8,128)(2,1)} %get-tuple-element.16) | data formatting | bytes 4194304
  88.7 0.0 copy-done
  88.7 0.0 copy-start.1
  88.7 0.0 copy-start.2
  88.7 1.3 %copy.14 = bf16[128,8192]{1,0:T(8,128)(2,1)} copy(bf16[128,8192]{1,0:T(8,128)(2,1)S(1)} %copy-done) | data formatting | bytes 4194304
  90.0 0.1 copy-done.1
  90.1 0.8 copy.15
  90.9 0.0 copy-done.2
  90.9 0.6 copy.16
  (1 shorter events, 0.0 us)
Async XLA Ops:
  85.4 3.3 %copy-start = (bf16[128,8192]{1,0:T(8,128)(2,1)S(1)}, bf16[128,8192]{1,0:T(8,128)(2,1)}, u32[]{:S(2)}) copy-start(bf16[128,8192]{1,0:T(8,128)(2,1)} %get-tuple-element.17) | copy-start | bytes 6291460
  88.7 1.4 %copy-start.1 = (bf16[128,2048]{1,0:T(8,128)(2,1)S(1)}, bf16[128,2048]{1,0:T(8,128)(2,1)}, u32[]{:S(2)}) copy-start(bf16[128,2048]{1,0:T(8,128)(2,1)} %get-tuple-element.18) | copy-start | bytes 1572868
  88.7 2.2 %copy-start.2 = (f32[80,128]{1,0:T(8,128)S(1)}, f32[80,128]{1,0:T(8,128)}, u32[]{:S(2)}) copy-start(f32[80,128]{1,0:T(8,128)} %get-tuple-element.11) | copy-start | bytes 122884
where the time goes:
time: 91.7 us; the launch traced here: 91.5 us
  Pallas kernels  84.2 us (92%)
  local copies, waits for them, and re-layouts  6.04 us (7%)
    pallas_call x1, Pallas kernels, fused_shards(): pl.pallas_call(functools.partial(fused_kernel, n, ndp, rows), out_shape=(...  84.2 us
    unnamed x10, local copies, waits for them, and re-layouts  6.04 us

commit v1 on v0

--- a/solution.py
+++ b/solution.py
@@ -255,6 +255,7 @@
 
 MESH = pl.DeviceIdType.MESH
 D = HEAD_DIMENSION
+LOG2E = 1.4426950408889634
 NT = (((1,), (1,)), ((), ()))
 NN = (((1,), (0,)), ((), ()))
 
@@ -289,10 +290,17 @@
     pairs = KEY_VALUE_HEADS // 2
     copies = half // pairs
     wide = copies * D
+    steps = copies // 2
+    part_rows = tokens // 2
+    window = group // 2
     scale = D ** (-0.5)
     key_base = QUERY_HEADS * D
     value_base = key_base + KEY_VALUE_HEADS * D
     query_at = slice(home, span)
+    reach = [
+        (max(0, (home + u * part_rows - window + 1) // part_rows * part_rows), home + (u + 1) * part_rows)
+        for u in range(2)
+    ]
 
     def aligned(start, size):
         return pl.ds(pl.multiple_of(start, size), size)
@@ -323,15 +331,15 @@
             return pltpu.make_async_copy(src, dst, kv_recv.at[kind, j, 0])
         return move(src, dst, kv_send.at[kind, j, o], kv_recv.at[kind, j, o], peer)
 
-    def query_in(j, o):
+    def query_in(g, o):
         peer = sp_peer(o)
         src = out_q.at[
-            pl.ds(lax.rem(peer, 2) * half + j * copies, copies), aligned(peer // 2 * share, share), :
+            pl.ds(lax.rem(peer, 2) * half + g * 2, 2), aligned(peer // 2 * share, share), :
         ]
-        dst = recv_q.at[pl.ds(j * copies, copies), aligned(me * share, share), :]
+        dst = recv_q.at[pl.ds(g * 2, 2), aligned(me * share, share), :]
         if o == 0:
-            return pltpu.make_async_copy(src, dst, q_recv.at[j, 0])
-        return move(src, dst, q_send.at[j, o], q_recv.at[j, o], peer)
+            return pltpu.make_async_copy(src, dst, q_recv.at[g, 0])
+        return move(src, dst, q_send.at[g, o], q_recv.at[g, o], peer)
 
     def upstream_in(j, here):
         who = core if here else 1 - core
@@ -417,8 +425,9 @@
             ordered = dot(perm_out[...], proj_ref[:, columns(first * D, wide)])
             for i in range(copies):
                 out_q[first + i] = ordered[:, i * D : (i + 1) * D].astype(jnp.bfloat16)
-        for o in range(n):
-            query_in(j, o).start()
+        for step in range(steps):
+            for o in range(n):
+                query_in(j * steps + step, o).start()
         return carry
 
     lax.fori_loop(0, pairs, send_pair, 0)
@@ -449,12 +458,19 @@
 
     lax.fori_loop(0, span // 128, table_block, 0)
 
-    query_token = lax.broadcasted_iota(jnp.int32, (1, tokens), 1) + chip * tokens
-    query_first = first_of(query_token)
+    for u in range(2):
+        first_key, last_key = reach[u]
+        lane = lax.broadcasted_iota(jnp.int32, (1, tokens), 1)
+        lane = jnp.where(lane >= part_rows, lane - part_rows, lane)
+        query_token = lane + (chip * tokens + u * part_rows)
+        query_first = first_of(query_token)
+        for part in range(first_key, last_key, part_rows):
+            key_token = lax.broadcasted_iota(jnp.int32, (part_rows, tokens), 0) + (low + part)
+            keep = (key_token >= query_first) & (key_token <= query_token)
+            mask_t[u, part - first_key : part - first_key + part_rows, :] = jnp.where(
+                keep, 0.0, -jnp.inf
+            )
     for w in range(back + 1):
-        key_token = lax.broadcasted_iota(jnp.int32, (tokens, tokens), 0) + (low + w * tokens)
-        keep = (key_token >= query_first) & (key_token <= query_token)
-        mask_t[w * tokens : (w + 1) * tokens, :] = jnp.where(keep, 0.0, -jnp.inf)
         for i in range(2 * pages_dev):
             at = jnp.maximum((chip - back + w) * 2 * pages_dev + i, 0)
             source = lax.div(page_ref[0, at], pages_dev)
@@ -483,50 +499,64 @@
         value_bias = bias_ref[pl.ds(QUERY_HEADS + KEY_VALUE_HEADS + core * pairs + j, 1), :]
         for w in range(back + 1):
             at = slice(w * tokens, (w + 1) * tokens)
-            rotated = rope(dot(perm_kv[at, :], recv_kv[0, j]) + key_bias, at)
+            pair = dot(perm_kv[at, :], jnp.concatenate([recv_kv[0, j], recv_kv[1, j]], 1))
+            rotated = rope(pair[:, :D] + key_bias, at)
             key_rows[at, :] = rotated.astype(jnp.bfloat16)
             key_t[:, at] = rotated.T.astype(jnp.bfloat16)
-            shifted = dot(perm_kv[at, :], recv_kv[1, j]) + value_bias
+            shifted = pair[:, D:] + value_bias
             value_rows[at, :] = shifted.astype(jnp.bfloat16)
             value_t[:, at] = shifted.T.astype(jnp.bfloat16)
         dk[...] = jnp.zeros_like(dk)
         dv[...] = jnp.zeros_like(dv)
-        for o in range(n):
-            copy = query_in(j, o)
-            copy.wait() if o == 0 else copy.wait_recv()
         upstream_in(j, True).wait()
         upstream_in(j, False).wait_recv()
 
         def two_heads(step, inner):
+            g = j * steps + step
+            for o in range(n):
+                copy = query_in(g, o)
+                copy.wait() if o == 0 else copy.wait_recv()
+            cols = [columns((g * 2 + part) * D, D) for part in range(2)]
+            both = dot(perm_q[...], jnp.concatenate([recv_q[g * 2], recv_q[g * 2 + 1]], 1))
+            queries = []
             for part in range(2):
-                h = j * copies + step * 2 + part
-                cols = columns(h * D, D)
-                query_bias = bias_ref[pl.ds(core * half + h, 1), :]
-                query = rope(dot(perm_q[...], recv_q[h]) + query_bias, query_at)
-                query = query.astype(jnp.bfloat16)
-                upstream = recv_c[:, cols]
+                query_bias = bias_ref[pl.ds(core * half + g * 2 + part, 1), :]
+                rotated = rope(both[:, part * D : (part + 1) * D] + query_bias, query_at)
+                queries.append(rotated.astype(jnp.bfloat16))
+            column_sums = [jnp.zeros((1, D), jnp.float32) for part in range(2)]
+            for u in range(2):
+                at = slice(u * part_rows, (u + 1) * part_rows)
+                table_at = slice(home + u * part_rows, home + (u + 1) * part_rows)
+                keys = slice(*reach[u])
+                query = jnp.concatenate([queries[0][at], queries[1][at]], 0)
+                upstream = jnp.concatenate([recv_c[at, cols[0]], recv_c[at, cols[1]]], 0)
                 upstream_t = upstream.astype(jnp.float32).T
-                scores = dot(key_rows[...], query, NT) * scale
-                weights = jnp.exp(scores + mask_t[...])
+                scores = dot(key_rows[keys, :], query, NT) * (scale * LOG2E)
+                weights = jnp.exp2(scores + mask_t[u])
                 totals = jnp.sum(weights, 0, keepdims=True)
                 shrink = jnp.where(totals > 1e37, 0.015625, 1.0)
                 probs = (weights * shrink) * (1.0 / (totals * shrink))
                 rounded = probs.astype(jnp.bfloat16)
-                attended_t = dot(value_t[...], rounded)
-                att_buf[:, cols] = attended_t.T.astype(jnp.bfloat16)
+                attended_t = dot(value_t[:, keys], rounded)
+                attended = attended_t.T.astype(jnp.bfloat16)
                 kept = attended_t.astype(jnp.bfloat16).astype(jnp.float32)
                 delta = jnp.sum(upstream_t * kept, 0, keepdims=True)
-                dprobs = dot(value_rows[...], upstream, NT)
+                dprobs = dot(value_rows[keys, :], upstream, NT)
                 dscores = (probs * (dprobs - delta)).astype(jnp.bfloat16)
-                grad_query = unrope(dot(key_t[...], dscores).T * scale, query_at)
-                grad_query = grad_query.astype(jnp.bfloat16)
-                gq_buf[:, cols] = grad_query
-                sums[pl.ds(h, 1), :] = jnp.sum(grad_query.astype(jnp.float32), 0, keepdims=True)
-                dk[...] += dot(dscores, query)
-                dv[...] += dot(rounded, upstream)
+                rot_query = dot(key_t[:, keys], dscores).T * scale
+                for part in range(2):
+                    rows_at = slice(part * part_rows, (part + 1) * part_rows)
+                    att_buf[at, cols[part]] = attended[rows_at]
+                    grad_query = unrope(rot_query[rows_at], table_at).astype(jnp.bfloat16)
+                    gq_buf[at, cols[part]] = grad_query
+                    column_sums[part] += jnp.sum(grad_query.astype(jnp.float32), 0, keepdims=True)
+                dk[keys, :] += dot(dscores, query)
+                dv[keys, :] += dot(rounded, upstream)
+            for part in range(2):
+                sums[pl.ds(g * 2 + part, 1), :] = column_sums[part]
             return inner
 
-        lax.fori_loop(0, copies // 2, two_heads, 0)
+        lax.fori_loop(0, steps, two_heads, 0)
         for w in range(back):
             at = slice(w * tokens, (w + 1) * tokens)
             part_kv[j, w, 0] = dk[at, :].astype(jnp.bfloat16)
@@ -596,7 +626,8 @@
         for o in range(1, n):
             for kind in range(2):
                 pair_in(kind, j, o).wait_send()
-            query_in(j, o).wait_send()
+            for step in range(steps):
+                query_in(j * steps + step, o).wait_send()
         upstream_in(j, False).wait_send()
         for kind in range(2):
             head_out(kind, j, True).wait()
@@ -623,6 +654,7 @@
     half = QUERY_HEADS // 2
     pairs = KEY_VALUE_HEADS // 2
     share = 2 * PAGE
+    reach = (group // 2 - 1 + rows - 1) // rows * rows + rows
     exponent = jnp.arange(D // 2, dtype=jnp.float32) * 2.0 / D
     frequency = jnp.power(jnp.float32(rope_base), -exponent)
     frequency = jnp.concatenate([frequency, frequency])[None, :]
@@ -657,7 +689,7 @@
             pltpu.VMEM((D, span), bf16),
             pltpu.VMEM((span, D), f32),
             pltpu.VMEM((span, D), f32),
-            pltpu.VMEM((span, tokens), f32),
+            pltpu.VMEM((2, reach, tokens), f32),
             pltpu.VMEM((tokens, half * D), bf16),
             pltpu.VMEM((tokens, half * D), bf16),
             pltpu.VMEM((span, D), f32),
@@ -670,7 +702,7 @@
             pltpu.VMEM((ndp, sum_rows, D), f32),
             pltpu.VMEM((sum_rows, D), f32),
             pltpu.VMEM((n, sum_rows, D), f32),
-            dma((2, pairs, n)), dma((2, pairs, n)), dma((pairs, n)), dma((pairs, n)),
+            dma((2, pairs, n)), dma((2, pairs, n)), dma((half // 2, n)), dma((half // 2, n)),
             dma((pairs,)), dma((pairs,)), dma((pairs,)),
             dma((2, pairs)), dma((2, pairs)), dma((2, pairs)),
             dma((pairs, back)), dma((pairs, back)),

time: 91.7 us -> 91.6 us (level)
  no operation moved by 1% of the time
where the time goes in v1:
time: 91.6 us; the launch traced here: 91.4 us
  Pallas kernels  84.1 us (92%)
  local copies, waits for them, and re-layouts  6.04 us (7%)
    pallas_call x1, Pallas kernels, fused_shards(): pl.pallas_call(functools.partial(fused_kernel, n, ndp, rows), out_shape=(...  84.1 us
    unnamed x10, local copies, waits for them, and re-layouts  6.04 us

profile of v1, /device:TPU:0, one launch (start us, length us, event | category | flops | bytes accessed | tf_op | source)
XLA Modules:
  0.0 91.4 jit_solution(2817939771685930250)
XLA Ops:
  0.6 0.6 maximum_bitcast_fusion.freq_ref
  1.2 84.1 %shard_map.84 = (bf16[128,8192]{1,0:T(8,128)(2,1)}, bf16[128,8192]{1,0:T(8,128)(2,1)}, bf16[128,2048]{1,0:T(8,128)(2,1)}, f32[80,128]{1,0:T(8,128)}) custom-call(s32[1,4]{1,0:T(1,128)} %len_ref.1, s32[1,64]{1,0:T(1,128)} %page_ref.1, bf16[128,10240]{1,0:T(8,128)(2,1)} %proj_ref.1, bf16[128,8192]{1,0:T(8,128)(2,1)} %cot_ref.1, f32[80,128]{1,0:T(8,128)} %bitcast.5, ...), custom_call_target="tpu_custom_call" | custom-call | flops 11274289152 | bytes 18874368 | tf_op jit(solution)/shard_map/pallas_call | solution.py:667
  85.3 0.0 copy-start
  85.4 3.2 %copy.13 = bf16[128,8192]{1,0:T(8,128)(2,1)} copy(bf16[128,8192]{1,0:T(8,128)(2,1)} %get-tuple-element.16) | data formatting | bytes 4194304
  88.6 0.0 copy-done
  88.6 0.0 copy-start.1
  88.6 0.0 copy-start.2
  88.6 1.3 %copy.14 = bf16[128,8192]{1,0:T(8,128)(2,1)} copy(bf16[128,8192]{1,0:T(8,128)(2,1)S(1)} %copy-done) | data formatting | bytes 4194304
  89.9 0.1 copy-done.1
  90.0 0.8 copy.15
  90.8 0.0 copy-done.2
  90.8 0.6 copy.16
  (1 shorter events, 0.0 us)
Async XLA Ops:
  85.3 3.3 %copy-start = (bf16[128,8192]{1,0:T(8,128)(2,1)S(1)}, bf16[128,8192]{1,0:T(8,128)(2,1)}, u32[]{:S(2)}) copy-start(bf16[128,8192]{1,0:T(8,128)(2,1)} %get-tuple-element.17) | copy-start | bytes 6291460
  88.6 1.4 %copy-start.1 = (bf16[128,2048]{1,0:T(8,128)(2,1)S(1)}, bf16[128,2048]{1,0:T(8,128)(2,1)}, u32[]{:S(2)}) copy-start(bf16[128,2048]{1,0:T(8,128)(2,1)} %get-tuple-element.18) | copy-start | bytes 1572868
  88.6 2.2 %copy-start.2 = (f32[80,128]{1,0:T(8,128)S(1)}, f32[80,128]{1,0:T(8,128)}, u32[]{:S(2)}) copy-start(f32[80,128]{1,0:T(8,128)} %get-tuple-element.11) | copy-start | bytes 122884
